TPU v7x, 32 devices: a whole 2x2x4 slice. The times are simulated.
32 devices in a mesh: groups: 2 (over y), blk: 4 (over z), op: 2 (over x), sub: 2 (over core).
Axes of the slice: x: 2, y: 2, z: 4, core: 2. Of those that a mesh axis runs over, the one named last changes fastest.
Arguments:
- wavefunction: bfloat16 [32, 512, 512], P(('groups', 'blk'), 'sub'), parts along dimension 0, may hold values from -6 to 6
- left_ops: bfloat16 [256, 512, 512], P(('groups', 'blk', 'op'), 'sub'), parts along dimension 0, may hold values from -0.25 to 0.25
- right_ops: bfloat16 [256, 512, 512], P(('groups', 'blk', 'op'), 'sub'), parts along dimension 0, may hold values from -0.25 to 0.25
- src_local: int32 [256], P(('groups', 'blk', 'op')), parts along dimension 0, may hold values from 0 to 3
- dst_dev: int32 [256, 1], P(('groups', 'blk', 'op')), parts along dimension 0, may hold values from 0 to 3; in each aligned block of 16 rows (0 to 15, 16 to 31, ...) at most 8 rows name the same one
- dst_local: int32 [256], P(('groups', 'blk', 'op')), parts along dimension 0, may hold values from 0 to 3
- row_counts: int32 [32], P('groups'), parts along dimension 0, may hold values from 1 to 512, 4096 in all
- col_counts: int32 [32], P('groups'), parts along dimension 0, may hold values from 1 to 512, 4096 in all
Outputs:
- hpsi: float32 [32, 512, 512], P(('groups', 'blk'), 'sub', 'op'), parts along dimension 0
There are 2 independent parts, one for each index of `groups`. A program takes and returns all parts, laid end to end along the dimension named above; each array names one. Nothing has to cross between parts.
Inputs may be any that keep to these rules, and one draw needn't show every extreme that they name: `dst_dev`: among the 16 pairs of one device at most 8 name the same blk index, and some device reaches 8. `row_counts`: they sum to 4096 and the largest is 512. `col_counts`: they sum to 4096 and the largest is 512.
All inputs are finite; a program needn't handle non-finite values.
Results may differ from a plain program's by a relative error of at most 0.0041.
Values may be sent and summed in bfloat16 or wider, within the bound.
A program may use at most 128 MiB of HBM per device.

v0:
```python
import jax
import jax.numpy as jnp
from jax import lax
from jax.sharding import PartitionSpec as P


def local(wavefunction, left_ops, right_ops, src_local, dst_dev, dst_local, row_counts, col_counts):
    num_blocks, half_rows, col_width = wavefunction.shape
    pairs_here = left_ops.shape[0]
    blk_count = lax.axis_size("blk")
    op_count = lax.axis_size("op")
    slots_per = 2 * pairs_here // blk_count
    piece_width = col_width // op_count
    sub_index = lax.axis_index("sub")
    blk_index = lax.axis_index("blk")
    op_index = lax.axis_index("op")
    first_block = blk_index * num_blocks
    my_rows = lax.dynamic_slice_in_dim(row_counts, first_block, num_blocks)
    my_cols = lax.dynamic_slice_in_dim(col_counts, first_block, num_blocks)
    row_ids = sub_index * half_rows + jnp.arange(half_rows, dtype=jnp.int32)
    col_ids = jnp.arange(col_width, dtype=jnp.int32)
    keep_mask = (row_ids[None, :, None] < my_rows[:, None, None]) & (
        col_ids[None, None, :] < my_cols[:, None, None]
    )
    masked = jnp.where(keep_mask, wavefunction, jnp.zeros((), jnp.bfloat16))
    chosen = jnp.take(lax.all_gather(masked, "sub", axis=1, tiled=True), src_local, axis=0)
    left_done = jnp.einsum(
        "pik,pkj->pij", left_ops, chosen, preferred_element_type=jnp.float32
    ).astype(jnp.bfloat16)
    products = jnp.einsum(
        "pik,pck->pic",
        left_done,
        lax.all_gather(right_ops, "sub", axis=1, tiled=True),
        preferred_element_type=jnp.float32,
    ).astype(jnp.bfloat16)
    target = dst_dev[:, 0]
    onehot = (target[:, None] == jnp.arange(blk_count, dtype=jnp.int32)[None, :]).astype(jnp.int32)
    earlier = jnp.cumsum(onehot, axis=0) - onehot
    slot_rank = jnp.sum(earlier * onehot, axis=1)
    slot_index = target * slots_per + slot_rank
    placing = jnp.arange(blk_count * slots_per, dtype=jnp.int32)[:, None] == slot_index[None, :]
    slot_ids = jnp.sum(placing.astype(jnp.int32) * (dst_local[None, :] + 1), axis=1) - 1
    slot_ids = slot_ids.reshape(blk_count, slots_per)
    placing = placing.astype(jnp.bfloat16).reshape(blk_count, slots_per, pairs_here)
    local_blocks = jnp.arange(num_blocks, dtype=jnp.int32)
    outgoing = jnp.einsum(
        "ncp,pix->ncix", placing, products, preferred_element_type=jnp.float32
    ).astype(jnp.bfloat16)
    arrived, arrived_ids = (
        lax.all_to_all(outgoing, "blk", split_axis=0, concat_axis=0, tiled=True),
        lax.all_to_all(slot_ids, "blk", split_axis=0, concat_axis=0, tiled=True),
    )
    select = (arrived_ids[None] == local_blocks[:, None, None]).astype(jnp.bfloat16)
    partial_sum = jnp.einsum("bnc,ncix->bix", select, arrived, preferred_element_type=jnp.float32)
    whole_sum = lax.psum(partial_sum, "op")
    result = lax.dynamic_slice_in_dim(whole_sum, op_index * piece_width, piece_width, 2)
    out_cols = op_index * piece_width + jnp.arange(piece_width, dtype=jnp.int32)
    keep_out = (row_ids[None, :, None] < my_rows[:, None, None]) & (
        out_cols[None, None, :] < my_cols[:, None, None]
    )
    return jnp.where(keep_out, result, jnp.zeros((), jnp.float32))


def solution(mesh):
    placed = (
        P(("groups", "blk"), "sub", None),
        P(("groups", "blk", "op"), "sub", None),
        P(("groups", "blk", "op"), "sub", None),
        P(("groups", "blk", "op")),
        P(("groups", "blk", "op"), None),
        P(("groups", "blk", "op")),
        P("groups"),
        P("groups"),
    )
    return jax.shard_map(
        local,
        mesh=mesh,
        in_specs=placed,
        out_specs=P(("groups", "blk"), "sub", "op"),
        check_vma=False,
    )
```

profile of v0, /device:TPU:0, one launch (start us, length us, event | category | flops | bytes accessed | tf_op | source)
XLA Modules:
  0.0 328.8 jit_solution(5626200889285133479)
XLA Ops:
  6.5 0.0 all-gather.3.cloned.1.call-start
  6.5 0.7 dynamic_slice.9
  7.3 0.7 dynamic_slice.10
  8.0 0.1 iota_compare_fusion
  8.1 0.1 broadcast_compare_fusion.1
  8.1 2.6 and_select_fusion
  10.7 0.0 all-gather.3.cloned.1.call-update
  10.7 0.0 all-gather.5.cloned.1.call-start
  10.8 0.7 all-gather.5.cloned.1.call-update
  11.5 0.7 fusion.19
  12.3 0.8 select_reduce_fusion.1
  13.1 0.7 broadcast_add_fusion.1
  13.8 0.7 multiply_add_fusion.1
  14.4 0.1 select_reduce_fusion
  14.5 0.7 sub.11
  15.2 6.3 %all-to-all-start = ((s32[4,1,8]{2,1,0:T(1,128)}), s32[4,1,8]{2,1,0:T(1,128)S(1)}, u32[]{:S(2)}, u32[]{:S(2)}) async-start(s32[4,1,8]{2,1,0:T(1,128)} %bitcast.1), calls=%async_computation | async-start | bytes 4096 | tf_op jit(solution)/shard_map/all_to_all | solution.py:51
  21.5 0.0 all-reduce.2.cloned.1.call-start
  21.5 0.7 compare_select_fusion
  22.2 0.7 compare_and_fusion
  22.8 1.3 all-gather.3.cloned.1.call-done
  24.2 6.3 %gather_fusion = bf16[16,512,512]{2,1,0:T(8,128)(2,1)} fusion(bf16[4,512,512]{2,1,0:T(8,128)(2,1)} %all-gather.3.cloned.1.call-done, s32[1024]{0:T(1024)S(1)} %pad_clamp_fusion), kind=kCustom, calls=%fused_computation | custom fusion | bytes 16777280 | tf_op jit(solution)/shard_map/jit(_take)/gather | solution.py:26
  30.4 16.3 %all-gather.5.cloned.1.call-done = bf16[16,512,512]{2,1,0:T(8,128)(2,1)} async-done(((bf16[16,256,512]{2,1,0:T(8,128)(2,1)}), bf16[16,512,512]{2,1,0:T(8,128)(2,1)}) %all-gather.5.cloned.1.call-update) | async-done | bytes 8388624 | tf_op jit(solution)/shard_map/all_gather | solution.py:33
  46.8 10.9 %fusion.8 = bf16[16,256,512]{2,1,0:T(8,128)(2,1)} fusion(bf16[16,512,512]{2,1,0:T(8,128)(2,1)} %all-gather.5.cloned.1.call-done, bf16[16,256,512]{2,1,0:T(8,128)(2,1)} %param.9, bf16[16,512,512]{2,1,0:T(8,128)(2,1)} %gather_fusion, pred[16]{0:T(512)(128)(4,1)S(1)} %compare_and_fusion), kind=kOutput, calls=%fused_computation.10 | convolution fusion | flops 4303355904 | bytes 25165840 | tf_op jit(solution)/shard_map/pik,pck->pic/dot_general | solution.py:30
  57.7 8.3 %convolution_convert_fusion = bf16[4,8,256,512]{3,1,2,0:T(8,128)(2,1)} fusion(bf16[16,256,512]{2,1,0:T(8,128)(2,1)} %fusion.8, s32[16]{0:T(128)S(1)} %multiply_add_fusion.1, s32[4,8]{1,0:T(4,128)S(1)} %multiply_add_fusion), kind=kOutput, calls=%fused_computation.4 | convolution fusion | flops 138412544 | bytes 12583104 | tf_op jit(solution)/shard_map/ncp,pix->ncix/dot_general | solution.py:46
  66.0 0.0 all-to-all-done
  66.0 188.3 %all_to_all.11 = bf16[4,8,256,512]{3,1,2,0:T(8,128)(2,1)S(1)} all-to-all(bf16[4,8,256,512]{3,1,2,0:T(8,128)(2,1)} %convolution_convert_fusion), channel_id=1, replica_groups=mesh['groups'=2,'blk'=4,'op'=2,'sub'=2] {'blk'}, dimensions={0} | all-to-all | bytes 16777216 | tf_op jit(solution)/shard_map/all_to_all | solution.py:50
  254.4 3.1 convolution_bitcast_fusion
  257.5 0.0 all-reduce.2.cloned.1.call-update
  257.5 0.2 copy.22
  257.7 0.1 broadcast_compare_fusion
  257.8 61.8 %all-reduce.2.cloned.1.call-done = f32[4,256,512]{2,0,1:T(4,128)} async-done(((f32[4,256,512]{2,0,1:T(4,128)}), f32[4,256,512]{2,0,1:T(4,128)}) %all-reduce.2.cloned.1.call-update) | async-done | bytes 2097168 | tf_op jit(solution)/shard_map/psum | solution.py:55
  319.6 1.5 dynamic-slice_select_fusion
  321.1 1.2 copy.28
  (6 shorter events, 0.1 us)
Async XLA Ops:
  6.5 17.6 %all-gather.3.cloned.1.call-start = ((), (), s32[]{:S(2)}) async-start(), calls=%async_computation.2 | async-start | bytes 3145728 | tf_op jit(solution)/shard_map/all_gather | solution.py:26
  10.7 36.0 %all-gather.5.cloned.1.call-start = ((), (), s32[]{:S(2)}) async-start(), calls=%async_computation.3 | async-start | bytes 12582912 | tf_op jit(solution)/shard_map/all_gather | solution.py:33
  15.2 50.9 %all-to-all-start = ((s32[4,1,8]{2,1,0:T(1,128)}), s32[4,1,8]{2,1,0:T(1,128)S(1)}, u32[]{:S(2)}, u32[]{:S(2)}) async-start(s32[4,1,8]{2,1,0:T(1,128)} %bitcast.1), calls=%async_computation | async-start | bytes 4096 | tf_op jit(solution)/shard_map/all_to_all | solution.py:51
  21.5 298.1 %all-reduce.2.cloned.1.call-start = ((), (), s32[]{:S(2)}) async-start(), calls=%async_computation.4 | async-start | bytes 4194304 | tf_op jit(solution)/shard_map/psum | solution.py:55
Sparse Core Ops, SparseCore 0:
  10.9 13.2 all-gather.2
  25.7 21.0 all-gather.4
  257.6 61.9 all-reduce.1
where the time goes:
time: 329 us
  blocking collectives  188 us (57%)
  waiting for transfers between devices  80.2 us (24%)
  matrix products  22.4 us (7%)
  between operations  13.1 us (4%)
  local copies, waits for them, and re-layouts  9.72 us (3%)
  other arithmetic  8.66 us (3%)
  starting transfers between devices  6.36 us (2%)
    all_to_all x1, blocking collectives, local(): lax.all_to_all(outgoing, 'blk', split_axis=0, concat_axis=0, tiled=True)  188 us
    psum x1, waiting for transfers between devices, local(): whole_sum = lax.psum(partial_sum, 'op')  61.8 us
    all_gather x1, waiting for transfers between devices, local(): lax.all_gather(right_ops, 'sub', axis=1, tiled=True)  16.3 us
    dot_general x1, matrix products, local(): jnp.einsum('pik,pck->pic', left_done, lax.all_gather(right_ops, 'sub', ax...  10.9 us
    dot_general x1, matrix products, local(): jnp.einsum('ncp,pix->ncix', placing, products, preferred_element_type=jnp...  8.3 us
  transfers between devices with their start and end apart: 4, of which 3 were waited for; matrix products, arithmetic and copies ran while one was open for 9% of the time, Pallas kernels for 0%

commit v1 on v0

v1 whole, which is shorter than its diff:
```python
import functools

import jax
import jax.numpy as jnp
from jax import lax
from jax.experimental import pallas as pl
from jax.experimental.pallas import tpu as pltpu
from jax.sharding import PartitionSpec as P

MESH = pl.DeviceIdType.MESH


def dest_at(step, blk, count):
    low, high = blk, count - 1 - blk
    lead = jnp.abs(high - low)
    near = jnp.minimum(low, high)
    far = jnp.where(high >= low, count - 1 - step, step)
    later = jnp.maximum(step - lead, 0)
    reach = near - later // 2
    close = jnp.where(later % 2 == 0, blk + reach, blk - reach)
    return jnp.where(step < lead, far, close)


def kernel(
    count, wave_hbm, left_hbm, right_hbm, src, dst_dev, dst_local, row_counts, col_counts, out,
    wave, left, right, runs, xs, xr, zr, zq, prev, last,
    local_sem, left_sem, own_sem, wave_send, wave_recv, right_send, right_recv,
    x_send, x_recv, z_send, z_recv, q_recv,
):
    blk, op, sub = lax.axis_index("blk"), lax.axis_index("op"), lax.axis_index("sub")
    pairs, half, width = left.shape
    blocks = wave.shape[0]
    piece = xs.shape[2]
    targets = xs.shape[0]
    has_low, has_high = blk > 0, blk < count - 1
    mine = pl.ds(pl.multiple_of(sub * half, half), half)

    wave_local = pltpu.make_async_copy(wave_hbm, wave.at[:, mine], local_sem)
    wave_local.start()

    def left_copy(p):
        return pltpu.make_async_copy(left_hbm.at[p], left.at[p], left_sem.at[p])

    def right_copy(p):
        return pltpu.make_async_copy(right_hbm.at[p], right.at[p, mine], own_sem.at[p])

    @pl.loop(0, pairs)
    def _(p):
        left_copy(p).start()
        right_copy(p).start()

    barrier = pltpu.get_barrier_semaphore()
    pl.semaphore_signal(barrier, inc=1, device_id={"sub": 1 - sub}, device_id_type=MESH)
    pl.semaphore_signal(barrier, inc=1, device_id={"op": 1 - op}, device_id_type=MESH)

    @pl.when(has_low)
    def _():
        pl.semaphore_signal(barrier, inc=1, device_id={"blk": blk - 1}, device_id_type=MESH)

    @pl.when(has_high)
    def _():
        pl.semaphore_signal(barrier, inc=1, device_id={"blk": blk + 1}, device_id_type=MESH)

    pl.semaphore_wait(barrier, 2 + has_low.astype(jnp.int32) + has_high.astype(jnp.int32))

    wave_copy = pltpu.make_async_remote_copy(
        src_ref=wave_hbm, dst_ref=wave.at[:, mine], send_sem=wave_send, recv_sem=wave_recv,
        device_id={"sub": 1 - sub}, device_id_type=MESH,
    )
    wave_copy.start()

    def right_remote(p):
        return pltpu.make_async_remote_copy(
            src_ref=right_hbm.at[p], dst_ref=right.at[p, mine],
            send_sem=right_send.at[p], recv_sem=right_recv.at[p],
            device_id={"sub": 1 - sub}, device_id_type=MESH,
        )

    @pl.loop(0, pairs)
    def _(p):
        right_remote(p).start()

    goals = [dst_dev[p] * blocks + dst_local[p] for p in range(pairs)]
    for p in range(pairs):
        found = jnp.int32(0)
        for q in range(p):
            found = jnp.where(goals[q] == goals[p], q + 1, found)
        prev[p] = found

    @pl.loop(0, targets)
    def _(t):
        found = jnp.int32(0)
        for p in range(pairs):
            found = jnp.where(goals[p] == t, p + 1, found)
        last[t] = found

    runs[0] = jnp.zeros(runs.shape[1:], jnp.float32)

    wave_local.wait()
    wave_copy.wait()

    @pl.loop(0, blocks)
    def _(j):
        at = blk * blocks + j
        shape = wave.shape[1:]
        keep = (lax.broadcasted_iota(jnp.int32, shape, 0) < row_counts[at]) & (
            lax.broadcasted_iota(jnp.int32, shape, 1) < col_counts[at]
        )
        wave[j] = jnp.where(keep, wave[j].astype(jnp.float32), 0.0).astype(wave.dtype)

    @pl.loop(0, pairs)
    def _(p):
        left_copy(p).wait()
        done = jnp.dot(left[p], wave[src[p]], preferred_element_type=jnp.float32)
        done = done.astype(jnp.bfloat16)
        right_copy(p).wait()
        right_remote(p).wait_recv()
        product = lax.dot_general(
            done, right[p], (((1,), (1,)), ((), ())), preferred_element_type=jnp.float32
        ).astype(jnp.bfloat16)
        runs[p + 1] = product.astype(jnp.float32) + runs[prev[p]]

    own_cols = pl.ds(pl.multiple_of(op * piece, piece), piece)
    peer_cols = pl.ds(pl.multiple_of((1 - op) * piece, piece), piece)

    def x_copy(t):
        return pltpu.make_async_remote_copy(
            src_ref=xs.at[t], dst_ref=xr.at[t], send_sem=x_send.at[t], recv_sem=x_recv.at[t],
            device_id={"op": 1 - op}, device_id_type=MESH,
        )

    def z_copy(t, to):
        return pltpu.make_async_remote_copy(
            src_ref=xr.at[t], dst_ref=zr.at[t], send_sem=z_send.at[t], recv_sem=z_recv.at[t],
            device_id={"blk": to}, device_id_type=MESH,
        )

    def q_copy(t, j, to):
        return pltpu.make_async_remote_copy(
            src_ref=xr.at[t], dst_ref=zq.at[j], send_sem=z_send.at[t], recv_sem=q_recv.at[j],
            device_id={"blk": to}, device_id_type=MESH,
        )

    @pl.loop(0, targets)
    def _(i):
        t = dest_at(i // blocks, blk, count) * blocks + i % blocks
        xs[t] = runs[last[t], :, peer_cols].astype(xs.dtype)
        x_copy(t).start()

    @pl.loop(0, targets - blocks)
    def _(i):
        owner = dest_at(i // blocks, blk, count)
        j = i % blocks
        t = owner * blocks + j
        x_copy(t).wait_recv()
        up = owner > blk
        follows = (up & has_low) | (jnp.logical_not(up) & has_high)

        @pl.when(follows)
        def _():
            z_copy(t, blk).wait_recv()
            xr[t] = (
                runs[last[t], :, own_cols] + xr[t].astype(jnp.float32) + zr[t].astype(jnp.float32)
            ).astype(xr.dtype)

        @pl.when(jnp.logical_not(follows))
        def _():
            xr[t] = (runs[last[t], :, own_cols] + xr[t].astype(jnp.float32)).astype(xr.dtype)

        @pl.when(up)
        def _():
            z_copy(t, blk + 1).start()

        @pl.when(owner < blk - 1)
        def _():
            z_copy(t, blk - 1).start()

        @pl.when(owner == blk - 1)
        def _():
            q_copy(t, j, blk - 1).start()

    @pl.loop(0, blocks)
    def _(j):
        t = blk * blocks + j
        x_copy(t).wait_recv()
        out[j] = runs[last[t], :, own_cols] + xr[t].astype(jnp.float32)

        @pl.when(has_low)
        def _():
            z_copy(t, blk).wait_recv()
            out[j] += zr[t].astype(jnp.float32)

        @pl.when(has_high)
        def _():
            q_copy(t, j, blk).wait_recv()
            out[j] += zq[j].astype(jnp.float32)

        shape = out.shape[1:]
        keep = (lax.broadcasted_iota(jnp.int32, shape, 0) + sub * half < row_counts[t]) & (
            lax.broadcasted_iota(jnp.int32, shape, 1) + op * piece < col_counts[t]
        )
        out[j] = jnp.where(keep, out[j], 0.0)

    @pl.loop(0, pairs)
    def _(p):
        right_remote(p).wait_send()

    @pl.loop(0, targets)
    def _(t):
        x_copy(t).wait_send()

        @pl.when(t // blocks != blk)
        def _():
            z_copy(t, blk).wait_send()


def local(wavefunction, left_ops, right_ops, src_local, dst_dev, dst_local, row_counts, col_counts):
    blocks, half, width = wavefunction.shape
    pairs = left_ops.shape[0]
    count, op_count = lax.axis_size("blk"), lax.axis_size("op")
    piece = width // op_count
    targets = count * blocks
    small = pltpu.VMEM((targets, half, piece), jnp.bfloat16)
    dma = pltpu.SemaphoreType.DMA
    return pl.pallas_call(
        functools.partial(kernel, count),
        out_shape=jax.ShapeDtypeStruct((blocks, half, piece), jnp.float32),
        in_specs=[pl.BlockSpec(memory_space=pl.ANY)] * 3 + [pl.BlockSpec(memory_space=pltpu.SMEM)] * 5,
        out_specs=pl.BlockSpec(memory_space=pltpu.VMEM),
        scratch_shapes=[
            pltpu.VMEM((blocks, 2 * half, width), jnp.bfloat16),
            pltpu.VMEM((pairs, half, width), jnp.bfloat16),
            pltpu.VMEM((pairs, 2 * half, width), jnp.bfloat16),
            pltpu.VMEM((pairs + 1, half, width), jnp.float32),
            small,
            small,
            small,
            pltpu.VMEM((blocks, half, piece), jnp.bfloat16),
            pltpu.SMEM((pairs,), jnp.int32),
            pltpu.SMEM((targets,), jnp.int32),
            dma,
            dma((pairs,)),
            dma((pairs,)),
            dma,
            dma,
            dma((pairs,)),
            dma((pairs,)),
            dma((targets,)),
            dma((targets,)),
            dma((targets,)),
            dma((targets,)),
            dma((blocks,)),
        ],
        compiler_params=pltpu.CompilerParams(
            collective_id=0, has_side_effects=True, vmem_limit_bytes=60 * 2**20
        ),
        cost_estimate=pl.CostEstimate(
            flops=4 * pairs * half * width * width * 2,
            bytes_accessed=2 * left_ops.size * 2 + 2 * wavefunction.size,
            transcendentals=0,
        ),
    )(
        wavefunction, left_ops, right_ops, src_local, dst_dev.reshape(pairs), dst_local,
        row_counts, col_counts,
    )


def solution(mesh):
    placed = (
        P(("groups", "blk"), "sub", None),
        P(("groups", "blk", "op"), "sub", None),
        P(("groups", "blk", "op"), "sub", None),
        P(("groups", "blk", "op")),
        P(("groups", "blk", "op"), None),
        P(("groups", "blk", "op")),
        P("groups"),
        P("groups"),
    )
    return jax.shard_map(
        local,
        mesh=mesh,
        in_specs=placed,
        out_specs=P(("groups", "blk"), "sub", "op"),
        check_vma=False,
    )
```

time: 329 us -> 70 us (0.21)
  blocking collectives: 188 us -> 0 us
  waiting for transfers between devices: 80.2 us -> 0 us
  Pallas kernels: 0 us -> 67.6 us
  matrix products: 22.4 us -> 0 us
  between operations: 13.1 us -> 0.01 us
  other arithmetic: 8.66 us -> 0 us
  local copies, waits for them, and re-layouts: 9.72 us -> 2.29 us
  starting transfers between devices: 6.36 us -> 0 us
    all_to_all x1 -> x0, blocking collectives: 188 us -> none  [local(): lax.all_to_all(outgoing, 'blk', split_axis=0, concat_axis=0, tiled=True)]
    pallas_call x0 -> x1, Pallas kernels: none -> 67.6 us  [local(): pl.pallas_call(functools.partial(kernel, count), out_shape=jax.ShapeDtype...]
    psum x1 -> x0, waiting for transfers between devices: 61.8 us -> none  [local(): whole_sum = lax.psum(partial_sum, 'op')]
    dot_general x3 -> x0, matrix products: 22.4 us -> none  [the longest x1 10.9 us: local(): jnp.einsum('pik,pck->pic', left_done, lax.all_gather(right_ops, 'sub', ax...]
    all_gather x2 -> x0, waiting for transfers between devices: 17.7 us -> none  [the longest x1 16.3 us: local(): lax.all_gather(right_ops, 'sub', axis=1, tiled=True)]
    all_to_all x1 -> x0, starting transfers between devices: 6.32 us -> none  [local(): lax.all_to_all(slot_ids, 'blk', split_axis=0, concat_axis=0, tiled=True)]
    gather x1 -> x0, local copies, waits for them, and re-layouts: 6.27 us -> none  [local(): jnp.take(lax.all_gather(masked, 'sub', axis=1, tiled=True), src_local, ax...]
    select_n x3 -> x0, other arithmetic: 4.74 us -> none  [the longest x1 2.57 us: local(): masked = jnp.where(keep_mask, wavefunction, jnp.zeros((), jnp.bfloat16))]
  transfers between devices with their start and end apart: 4 -> 0, of which waited for: 3 -> 0; matrix products, arithmetic and copies ran while one was open for 9% -> 0% of each run, Pallas kernels for 0% -> 0%
where the time goes in v1:
time: 70 us; the launch traced here: 69.9 us
  Pallas kernels  67.6 us (97%)
  local copies, waits for them, and re-layouts  2.29 us (3%)
    pallas_call x1, Pallas kernels, local(): pl.pallas_call(functools.partial(kernel, count), out_shape=jax.ShapeDtype...  67.6 us
    unnamed x1, local copies, waits for them, and re-layouts  2.29 us

profile of v1, /device:TPU:0, one launch (start us, length us, event | category | flops | bytes accessed | tf_op | source)
XLA Modules:
  0.0 69.9 jit_solution(15523559329799388032)
XLA Ops:
  0.0 67.6 %shard_map.82 = f32[4,256,256]{2,1,0:T(8,128)} custom-call(bf16[4,256,512]{2,1,0:T(8,128)(2,1)} %wave_hbm.1, bf16[16,256,512]{2,1,0:T(8,128)(2,1)} %left_hbm.1, bf16[16,256,512]{2,1,0:T(8,128)(2,1)} %right_hbm.1, s32[16]{0:T(128)} %src.1, s32[16]{0:T(128)} %bitcast.1, s32[16]{0:T(128)} %dst_local.1, s32[16]{0:T(128)} %row_counts.1, s32[16]{0:T(128)} %col_counts.1), custom_call_target="tpu_custom_call" | custom-call | flops 8589934592 | bytes 9437184 | tf_op jit(solution)/shard_map/pallas_call | solution.py:225
  67.6 2.3 %copy.10 = f32[4,256,256]{2,1,0:T(8,128)} copy(f32[4,256,256]{2,1,0:T(8,128)} %shard_map.82) | data formatting | bytes 2097152

commit v2 on v1

v2 whole, which is shorter than its diff:
```python
import functools

import jax
import jax.numpy as jnp
from jax import lax
from jax.experimental import pallas as pl
from jax.experimental.pallas import tpu as pltpu
from jax.sharding import PartitionSpec as P

MESH = pl.DeviceIdType.MESH


TILE = 32
GROUP = 8
LAG = 2
SLOTS = 4


def kernel(
    count, op_count, chunks,
    wave_hbm, left_hbm, right_hbm, src, dst_dev, dst_local, row_counts, col_counts, out,
    wave, left, right, runs, xs, xr, zr, zl, ro, lo, stage, got, prev, last, tiles, first, tile_of, tile_row, tile_run,
    local_sem, left_sem, own_sem, wave_send, wave_recv, left_send, left_recv,
    x_send, x_recv, r_send, r_recv, l_send, l_recv, out_send, out_recv,
):
    blk, op, sub = lax.axis_index("blk"), lax.axis_index("op"), lax.axis_index("sub")
    pairs, rows, width = left.shape
    half = rows // 2
    blocks = wave.shape[0]
    targets = count * blocks
    piece = out.shape[2]
    per_half = op_count // 2
    owner = op // per_half == sub
    has_low, has_high = blk > 0, blk < count - 1
    mine = pl.ds(pl.multiple_of(sub * half, half), half)

    wave_local = pltpu.make_async_copy(wave_hbm, wave.at[:, mine], local_sem)
    wave_local.start()

    def left_copy(p):
        return pltpu.make_async_copy(left_hbm.at[p], left.at[p, mine], left_sem.at[p])

    def right_copy(p):
        return pltpu.make_async_copy(right_hbm.at[p], right.at[p], own_sem.at[p])

    @pl.loop(0, pairs)
    def _(p):
        left_copy(p).start()
        right_copy(p).start()

    barrier = pltpu.get_barrier_semaphore()
    pl.semaphore_signal(barrier, inc=1, device_id={"sub": 1 - sub}, device_id_type=MESH)
    for step in range(1, op_count):
        pl.semaphore_signal(
            barrier, inc=1, device_id={"op": lax.rem(op + step, op_count)}, device_id_type=MESH
        )

    @pl.when(has_low)
    def _():
        pl.semaphore_signal(barrier, inc=1, device_id={"blk": blk - 1}, device_id_type=MESH)

    @pl.when(has_high)
    def _():
        pl.semaphore_signal(barrier, inc=1, device_id={"blk": blk + 1}, device_id_type=MESH)

    pl.semaphore_wait(barrier, op_count + has_low.astype(jnp.int32) + has_high.astype(jnp.int32))

    wave_copy = pltpu.make_async_remote_copy(
        src_ref=wave_hbm, dst_ref=wave.at[:, mine], send_sem=wave_send, recv_sem=wave_recv,
        device_id={"sub": 1 - sub}, device_id_type=MESH,
    )
    wave_copy.start()

    def left_remote(p):
        return pltpu.make_async_remote_copy(
            src_ref=left_hbm.at[p], dst_ref=left.at[p, mine],
            send_sem=left_send.at[p], recv_sem=left_recv.at[p],
            device_id={"sub": 1 - sub}, device_id_type=MESH,
        )

    @pl.loop(0, pairs)
    def _(p):
        left_remote(p).start()

    goals = [dst_dev[p] * blocks + dst_local[p] for p in range(pairs)]
    for p in range(pairs):
        found = jnp.int32(0)
        for q in range(p):
            found = jnp.where(goals[q] == goals[p], q + 1, found)
        prev[p] = found

    first[0] = 0

    @pl.loop(0, targets)
    def _(t):
        found = jnp.int32(0)
        for p in range(pairs):
            found = jnp.where(goals[p] == t, p + 1, found)
        last[t] = found
        tiles[t] = lax.div(row_counts[t] + (TILE - 1), TILE)
        first[t + 1] = first[t] + tiles[t]

    tile_of[0] = 0
    tile_row[0] = 0

    @pl.loop(0, chunks * GROUP)
    def _(k):
        t, r = tile_of[k], tile_row[k]
        over = r + 1 >= tiles[t]
        tile_of[k + 1] = jnp.where(over, jnp.minimum(t + 1, targets - 1), t)
        tile_row[k + 1] = jnp.where(over, 0, r + 1)
        tile_run[k] = last[t]

    runs[0] = jnp.zeros(runs.shape[1:], jnp.float32)

    wave_local.wait()
    wave_copy.wait()

    @pl.loop(0, blocks)
    def _(j):
        at = blk * blocks + j
        shape = wave.shape[1:]
        keep = (lax.broadcasted_iota(jnp.int32, shape, 0) < row_counts[at]) & (
            lax.broadcasted_iota(jnp.int32, shape, 1) < col_counts[at]
        )
        wave[j] = jnp.where(keep, wave[j].astype(jnp.float32), 0.0).astype(wave.dtype)

    @pl.loop(0, pairs)
    def _(p):
        left_copy(p).wait()
        left_remote(p).wait_recv()
        done = jnp.dot(left[p], wave[src[p]], preferred_element_type=jnp.float32)
        done = done.astype(jnp.bfloat16)
        right_copy(p).wait()
        product = lax.dot_general(
            done, right[p], (((1,), (1,)), ((), ())), preferred_element_type=jnp.float32
        ).astype(jnp.bfloat16)
        runs[p + 1] = product.astype(jnp.float32).reshape(runs.shape[1:]) + runs[prev[p]]

    def chunk_tiles(c):
        return pl.ds(c * GROUP, GROUP)

    def x_copy(h, c):
        to = sub * per_half + h
        slot = lax.rem(op - to + op_count - 1 + op_count, op_count)
        return pltpu.make_async_remote_copy(
            src_ref=xs.at[h, chunk_tiles(c)], dst_ref=xr.at[slot, chunk_tiles(c)],
            send_sem=x_send.at[h, c], recv_sem=x_recv.at[slot, c],
            device_id={"op": to}, device_id_type=MESH,
        )

    def x_wait(slot, c):
        pltpu.make_async_remote_copy(
            src_ref=xs.at[0, chunk_tiles(c)], dst_ref=xr.at[slot, chunk_tiles(c)],
            send_sem=x_send.at[0, c], recv_sem=x_recv.at[slot, c],
            device_id={"op": op}, device_id_type=MESH,
        ).wait_recv()

    def r_copy(c):
        return pltpu.make_async_remote_copy(
            src_ref=ro.at[lax.rem(c, SLOTS)], dst_ref=zr.at[chunk_tiles(c)],
            send_sem=r_send.at[c], recv_sem=r_recv.at[c],
            device_id={"blk": blk + 1}, device_id_type=MESH,
        )

    def l_copy(c):
        return pltpu.make_async_remote_copy(
            src_ref=lo.at[lax.rem(c, SLOTS)], dst_ref=zl.at[chunk_tiles(c)],
            send_sem=l_send.at[c], recv_sem=l_recv.at[c],
            device_id={"blk": blk - 1}, device_id_type=MESH,
        )

    def out_copy(j):
        return pltpu.make_async_remote_copy(
            src_ref=stage.at[j], dst_ref=got.at[j], send_sem=out_send.at[j], recv_sem=out_recv.at[j],
            device_id={"sub": 1 - sub}, device_id_type=MESH,
        )

    def send_chunk(c):
        for q in range(GROUP):
            k = c * GROUP + q
            for h in range(per_half):
                part = runs[tile_run[k], tile_row[k], :, h * piece:(h + 1) * piece]
                xs[h, k] = part.astype(xs.dtype)
        for h in range(per_half):

            @pl.when(sub * per_half + h != op)
            def _():
                x_copy(h, c).start()

    if op_count > 2:
        pl.loop(0, chunks)(send_chunk)
    else:

        @pl.when(jnp.logical_not(owner))
        def _():
            pl.loop(0, chunks)(send_chunk)

    def add_chunk(c):
        for slot in range(op_count - 1):
            x_wait(slot, c)
        own = pl.ds(pl.multiple_of(lax.rem(op, per_half) * piece, piece), piece)
        for q in range(GROUP):
            k = c * GROUP + q
            total = runs[tile_run[k], tile_row[k], :, own]
            for slot in range(op_count - 1):
                total += xr[slot, k].astype(jnp.float32)
            xr[0, k] = total.astype(xr.dtype)

    def pass_on(c, has_in, has_out, copy, arrived, slots):
        @pl.when((c >= 0) & (c < chunks))
        def _():
            @pl.when(has_in)
            def _():
                copy(c).wait_recv()

            @pl.when(has_out)
            def _():
                @pl.when(c >= SLOTS)
                def _():
                    copy(c - SLOTS).wait_send()

                @pl.when(has_in)
                def _():
                    slots[lax.rem(c, SLOTS)] = (
                        xr[0, chunk_tiles(c)].astype(jnp.float32)
                        + arrived[chunk_tiles(c)].astype(jnp.float32)
                    ).astype(slots.dtype)

                @pl.when(jnp.logical_not(has_in))
                def _():
                    slots[lax.rem(c, SLOTS)] = xr[0, chunk_tiles(c)]

                copy(c).start()

    def finish(j, side):
        t = blk * blocks + j
        for r in range(half // TILE):
            row = side * (half // TILE) + r
            at = jnp.minimum(first[t] + row, chunks * GROUP - 1)
            total = xr[0, at].astype(jnp.float32)
            total += jnp.where(has_low, zr[at].astype(jnp.float32), 0.0)
            total += jnp.where(has_high, zl[at].astype(jnp.float32), 0.0)
            shape = total.shape
            keep = (lax.broadcasted_iota(jnp.int32, shape, 0) + row * TILE < row_counts[t]) & (
                lax.broadcasted_iota(jnp.int32, shape, 1) + op * piece < col_counts[t]
            )
            yield r, jnp.where(keep, total, 0.0)

    @pl.when(owner)
    def _():
        @pl.loop(0, chunks + LAG * (count - 1))
        def _(i):
            @pl.when(i < chunks)
            def _():
                add_chunk(i)

            pass_on(i - LAG * blk, has_low, has_high, r_copy, zr, ro)
            pass_on(i - LAG * (count - 1 - blk), has_high, has_low, l_copy, zl, lo)

        @pl.loop(0, blocks)
        def _(j):
            for r, total in finish(j, 1 - sub):
                stage[j, r * TILE:(r + 1) * TILE] = total
            out_copy(j).start()

        @pl.loop(0, blocks)
        def _(j):
            for r, total in finish(j, sub):
                out[j, r * TILE:(r + 1) * TILE] = total

        @pl.loop(chunks - SLOTS, chunks)
        def _(c):
            @pl.when(has_high)
            def _():
                r_copy(c).wait_send()

            @pl.when(has_low)
            def _():
                l_copy(c).wait_send()

        @pl.loop(0, blocks)
        def _(j):
            out_copy(j).wait_send()

    @pl.when(jnp.logical_not(owner))
    def _():
        @pl.loop(0, blocks)
        def _(j):
            out_copy(j).wait_recv()
            out[j] = got[j]

    @pl.loop(0, pairs)
    def _(p):
        left_remote(p).wait_send()

    for h in range(per_half):

        @pl.when(sub * per_half + h != op)
        def _():
            @pl.loop(0, chunks)
            def _(c):
                x_copy(h, c).wait_send()


def local(wavefunction, left_ops, right_ops, src_local, dst_dev, dst_local, row_counts, col_counts):
    blocks, half, width = wavefunction.shape
    rows = 2 * half
    pairs = left_ops.shape[0]
    count, op_count = lax.axis_size("blk"), lax.axis_size("op")
    piece = width // op_count
    targets = count * blocks
    most = (targets * rows // 2 + targets * (TILE - 1)) // TILE
    chunks = -(-most // GROUP)
    packed = chunks * GROUP
    dma = pltpu.SemaphoreType.DMA
    bf16 = jnp.bfloat16
    return pl.pallas_call(
        functools.partial(kernel, count, op_count, chunks),
        out_shape=jax.ShapeDtypeStruct((blocks, half, piece), jnp.float32),
        in_specs=[pl.BlockSpec(memory_space=pl.ANY)] * 3 + [pl.BlockSpec(memory_space=pltpu.SMEM)] * 5,
        out_specs=pl.BlockSpec(memory_space=pltpu.VMEM),
        scratch_shapes=[
            pltpu.VMEM((blocks, rows, width), bf16),
            pltpu.VMEM((pairs, rows, width), bf16),
            pltpu.VMEM((pairs, half, width), bf16),
            pltpu.VMEM((pairs + 1, rows // TILE, TILE, width // 2), jnp.float32),
            pltpu.VMEM((op_count // 2, packed, TILE, piece), bf16),
            pltpu.VMEM((op_count - 1, packed, TILE, piece), bf16),
            pltpu.VMEM((packed, TILE, piece), bf16),
            pltpu.VMEM((packed, TILE, piece), bf16),
            pltpu.VMEM((SLOTS, GROUP, TILE, piece), bf16),
            pltpu.VMEM((SLOTS, GROUP, TILE, piece), bf16),
            pltpu.VMEM((blocks, half, piece), jnp.float32),
            pltpu.VMEM((blocks, half, piece), jnp.float32),
            pltpu.SMEM((pairs,), jnp.int32),
            pltpu.SMEM((targets,), jnp.int32),
            pltpu.SMEM((targets,), jnp.int32),
            pltpu.SMEM((targets + 1,), jnp.int32),
            pltpu.SMEM((chunks * GROUP + 1,), jnp.int32),
            pltpu.SMEM((chunks * GROUP + 1,), jnp.int32),
            pltpu.SMEM((chunks * GROUP,), jnp.int32),
            dma,
            dma((pairs,)),
            dma((pairs,)),
            dma,
            dma,
            dma((pairs,)),
            dma((pairs,)),
            dma((op_count // 2, chunks)),
            dma((op_count - 1, chunks)),
            dma((chunks,)),
            dma((chunks,)),
            dma((chunks,)),
            dma((chunks,)),
            dma((blocks,)),
            dma((blocks,)),
        ],
        compiler_params=pltpu.CompilerParams(
            collective_id=0, has_side_effects=True, vmem_limit_bytes=60 * 2**20
        ),
        cost_estimate=pl.CostEstimate(
            flops=6 * pairs * half * width * width * 2,
            bytes_accessed=2 * left_ops.size * 2 + 2 * wavefunction.size,
            transcendentals=0,
        ),
    )(
        wavefunction, left_ops, right_ops, src_local, dst_dev.reshape(pairs), dst_local,
        row_counts, col_counts,
    )


def solution(mesh):
    placed = (
        P(("groups", "blk"), "sub", None),
        P(("groups", "blk", "op"), "sub", None),
        P(("groups", "blk", "op"), "sub", None),
        P(("groups", "blk", "op")),
        P(("groups", "blk", "op"), None),
        P(("groups", "blk", "op")),
        P("groups"),
        P("groups"),
    )
    return jax.shard_map(
        local,
        mesh=mesh,
        in_specs=placed,
        out_specs=P(("groups", "blk"), "sub", "op"),
        check_vma=False,
    )
```

time: 70 us -> 78.7 us (1.12)
  Pallas kernels: 67.6 us -> 76.1 us
    pallas_call x1, Pallas kernels: 67.6 us -> 76.1 us  [local(): pl.pallas_call(functools.partial(kernel, count, op_count, chunks), out_sh...]
where the time goes in v2:
time: 78.7 us; the launch traced here: 78.4 us
  Pallas kernels  76.1 us (97%)
  local copies, waits for them, and re-layouts  2.29 us (3%)
    pallas_call x1, Pallas kernels, local(): pl.pallas_call(functools.partial(kernel, count, op_count, chunks), out_sh...  76.1 us
    unnamed x1, local copies, waits for them, and re-layouts  2.29 us

profile of v2, /device:TPU:0, one launch (start us, length us, event | category | flops | bytes accessed | tf_op | source)
XLA Modules:
  0.0 78.4 jit_solution(2896384341729803036)
XLA Ops:
  0.0 76.1 %shard_map.82 = f32[4,256,256]{2,1,0:T(8,128)} custom-call(bf16[4,256,512]{2,1,0:T(8,128)(2,1)} %wave_hbm.1, bf16[16,256,512]{2,1,0:T(8,128)(2,1)} %left_hbm.1, bf16[16,256,512]{2,1,0:T(8,128)(2,1)} %right_hbm.1, s32[16]{0:T(128)} %src.1, s32[16]{0:T(128)} %bitcast.1, s32[16]{0:T(128)} %dst_local.1, s32[16]{0:T(128)} %row_counts.1, s32[16]{0:T(128)} %col_counts.1), custom_call_target="tpu_custom_call" | custom-call | flops 12884901888 | bytes 9437184 | tf_op jit(solution)/shard_map/pallas_call | solution.py:318
  76.1 2.3 %copy.10 = f32[4,256,256]{2,1,0:T(8,128)} copy(f32[4,256,256]{2,1,0:T(8,128)} %shard_map.82) | data formatting | bytes 2097152

commit v3 on v2

--- a/solution.py
+++ b/solution.py
@@ -12,20 +12,20 @@
 
 TILE = 32
 GROUP = 8
-LAG = 2
+SKEW = 3
+AHEAD = 10
 SLOTS = 4
 
 
 def kernel(
     count, op_count, chunks,
     wave_hbm, left_hbm, right_hbm, src, dst_dev, dst_local, row_counts, col_counts, out,
-    wave, left, right, runs, xs, xr, zr, zl, ro, lo, stage, got, prev, last, tiles, first, tile_of, tile_row, tile_run,
-    local_sem, left_sem, own_sem, wave_send, wave_recv, left_send, left_recv,
-    x_send, x_recv, r_send, r_recv, l_send, l_recv, out_send, out_recv,
+    wave, done, right, runs, xs, xr, zin, zout, stage, got, prev, last, tiles, first, tile_of, tile_row, tile_run,
+    local_sem, left_sem, own_sem, wave_send, wave_recv, done_send, done_recv,
+    x_send, x_recv, t_send, t_recv, z_send, z_recv, out_send, out_recv,
 ):
     blk, op, sub = lax.axis_index("blk"), lax.axis_index("op"), lax.axis_index("sub")
-    pairs, rows, width = left.shape
-    half = rows // 2
+    pairs, half, width = right.shape
     blocks = wave.shape[0]
     targets = count * blocks
     piece = out.shape[2]
@@ -38,7 +38,7 @@
     wave_local.start()
 
     def left_copy(p):
-        return pltpu.make_async_copy(left_hbm.at[p], left.at[p, mine], left_sem.at[p])
+        return pltpu.make_async_copy(left_hbm.at[p], done.at[p, mine], left_sem.at[p])
 
     def right_copy(p):
         return pltpu.make_async_copy(right_hbm.at[p], right.at[p], own_sem.at[p])
@@ -71,16 +71,12 @@
     )
     wave_copy.start()
 
-    def left_remote(p):
+    def done_copy(p):
         return pltpu.make_async_remote_copy(
-            src_ref=left_hbm.at[p], dst_ref=left.at[p, mine],
-            send_sem=left_send.at[p], recv_sem=left_recv.at[p],
+            src_ref=done.at[p, mine], dst_ref=done.at[p, mine],
+            send_sem=done_send.at[p], recv_sem=done_recv.at[p],
             device_id={"sub": 1 - sub}, device_id_type=MESH,
         )
-
-    @pl.loop(0, pairs)
-    def _(p):
-        left_remote(p).start()
 
     goals = [dst_dev[p] * blocks + dst_local[p] for p in range(pairs)]
     for p in range(pairs):
@@ -128,12 +124,16 @@
     @pl.loop(0, pairs)
     def _(p):
         left_copy(p).wait()
-        left_remote(p).wait_recv()
-        done = jnp.dot(left[p], wave[src[p]], preferred_element_type=jnp.float32)
-        done = done.astype(jnp.bfloat16)
+        part = jnp.dot(done[p, mine], wave[src[p]], preferred_element_type=jnp.float32)
+        done[p, mine] = part.astype(done.dtype)
+        done_copy(p).start()
+
+    @pl.loop(0, pairs)
+    def _(p):
         right_copy(p).wait()
+        done_copy(p).wait_recv()
         product = lax.dot_general(
-            done, right[p], (((1,), (1,)), ((), ())), preferred_element_type=jnp.float32
+            done[p], right[p], (((1,), (1,)), ((), ())), preferred_element_type=jnp.float32
         ).astype(jnp.bfloat16)
         runs[p + 1] = product.astype(jnp.float32).reshape(runs.shape[1:]) + runs[prev[p]]
 
@@ -156,18 +156,18 @@
             device_id={"op": op}, device_id_type=MESH,
         ).wait_recv()
 
-    def r_copy(c):
+    def t_copy(c):
         return pltpu.make_async_remote_copy(
-            src_ref=ro.at[lax.rem(c, SLOTS)], dst_ref=zr.at[chunk_tiles(c)],
-            send_sem=r_send.at[c], recv_sem=r_recv.at[c],
-            device_id={"blk": blk + 1}, device_id_type=MESH,
-        )
-
-    def l_copy(c):
+            src_ref=xr.at[0, chunk_tiles(c)], dst_ref=xr.at[0, chunk_tiles(c)],
+            send_sem=t_send.at[c], recv_sem=t_recv.at[c],
+            device_id={"sub": 1 - sub}, device_id_type=MESH,
+        )
+
+    def z_copy(c, to):
         return pltpu.make_async_remote_copy(
-            src_ref=lo.at[lax.rem(c, SLOTS)], dst_ref=zl.at[chunk_tiles(c)],
-            send_sem=l_send.at[c], recv_sem=l_recv.at[c],
-            device_id={"blk": blk - 1}, device_id_type=MESH,
+            src_ref=zout.at[lax.rem(c, SLOTS)], dst_ref=zin.at[chunk_tiles(c)],
+            send_sem=z_send.at[c], recv_sem=z_recv.at[c],
+            device_id={"blk": to}, device_id_type=MESH,
         )
 
     def out_copy(j):
@@ -187,14 +187,6 @@
             @pl.when(sub * per_half + h != op)
             def _():
                 x_copy(h, c).start()
-
-    if op_count > 2:
-        pl.loop(0, chunks)(send_chunk)
-    else:
-
-        @pl.when(jnp.logical_not(owner))
-        def _():
-            pl.loop(0, chunks)(send_chunk)
 
     def add_chunk(c):
         for slot in range(op_count - 1):
@@ -206,93 +198,118 @@
             for slot in range(op_count - 1):
                 total += xr[slot, k].astype(jnp.float32)
             xr[0, k] = total.astype(xr.dtype)
-
-    def pass_on(c, has_in, has_out, copy, arrived, slots):
-        @pl.when((c >= 0) & (c < chunks))
-        def _():
+        t_copy(c).start()
+
+    def pass_on(c, has_in, has_out, to):
+        @pl.when(has_in)
+        def _():
+            z_copy(c, to).wait_recv()
+
+        @pl.when(has_out)
+        def _():
+            @pl.when(c >= SLOTS)
+            def _():
+                z_copy(c - SLOTS, to).wait_send()
+
             @pl.when(has_in)
             def _():
-                copy(c).wait_recv()
-
-            @pl.when(has_out)
-            def _():
-                @pl.when(c >= SLOTS)
-                def _():
-                    copy(c - SLOTS).wait_send()
-
-                @pl.when(has_in)
-                def _():
-                    slots[lax.rem(c, SLOTS)] = (
-                        xr[0, chunk_tiles(c)].astype(jnp.float32)
-                        + arrived[chunk_tiles(c)].astype(jnp.float32)
-                    ).astype(slots.dtype)
-
-                @pl.when(jnp.logical_not(has_in))
-                def _():
-                    slots[lax.rem(c, SLOTS)] = xr[0, chunk_tiles(c)]
-
-                copy(c).start()
-
-    def finish(j, side):
-        t = blk * blocks + j
-        for r in range(half // TILE):
-            row = side * (half // TILE) + r
-            at = jnp.minimum(first[t] + row, chunks * GROUP - 1)
-            total = xr[0, at].astype(jnp.float32)
-            total += jnp.where(has_low, zr[at].astype(jnp.float32), 0.0)
-            total += jnp.where(has_high, zl[at].astype(jnp.float32), 0.0)
-            shape = total.shape
-            keep = (lax.broadcasted_iota(jnp.int32, shape, 0) + row * TILE < row_counts[t]) & (
-                lax.broadcasted_iota(jnp.int32, shape, 1) + op * piece < col_counts[t]
-            )
-            yield r, jnp.where(keep, total, 0.0)
+                zout[lax.rem(c, SLOTS)] = (
+                    xr[0, chunk_tiles(c)].astype(jnp.float32)
+                    + zin[chunk_tiles(c)].astype(jnp.float32)
+                ).astype(zout.dtype)
+
+            @pl.when(jnp.logical_not(has_in))
+            def _():
+                zout[lax.rem(c, SLOTS)] = xr[0, chunk_tiles(c)]
+
+            z_copy(c, to).start()
+
+    def finish(has_in, has_got, has_out, to):
+        def tile(j, row):
+            return jnp.minimum(first[blk * blocks + j] + row, chunks * GROUP - 1)
+
+        steps = half // TILE
+
+        @pl.when(has_in)
+        def _():
+            @pl.loop(0, blocks)
+            def _(j):
+                for r in range(steps):
+                    stage[j, r * TILE:(r + 1) * TILE] = zin[tile(j, (1 - sub) * steps + r)]
+                out_copy(j).start()
+
+        @pl.loop(0, blocks)
+        def _(j):
+            @pl.when(has_got)
+            def _():
+                out_copy(j).wait_recv()
+
+            t = blk * blocks + j
+            for r in range(steps):
+                row = sub * steps + r
+                total = xr[0, tile(j, row)].astype(jnp.float32)
+                total += jnp.where(has_in, zin[tile(j, row)].astype(jnp.float32), 0.0)
+                given = got[j, r * TILE:(r + 1) * TILE].astype(jnp.float32)
+                total += jnp.where(has_got, given, 0.0)
+                shape = total.shape
+                keep = (
+                    lax.broadcasted_iota(jnp.int32, shape, 0) + row * TILE < row_counts[t]
+                ) & (lax.broadcasted_iota(jnp.int32, shape, 1) + op * piece < col_counts[t])
+                out[j, r * TILE:(r + 1) * TILE] = jnp.where(keep, total, 0.0)
+
+        @pl.when(has_in)
+        def _():
+            @pl.loop(0, blocks)
+            def _(j):
+                out_copy(j).wait_send()
+
+        @pl.when(has_out)
+        def _():
+            @pl.loop(chunks - SLOTS, chunks)
+            def _(c):
+                z_copy(c, to).wait_send()
 
     @pl.when(owner)
     def _():
-        @pl.loop(0, chunks + LAG * (count - 1))
+        if op_count > 2:
+            pl.loop(0, chunks)(send_chunk)
+
+        @pl.loop(0, chunks + SKEW * (count - 1))
         def _(i):
             @pl.when(i < chunks)
             def _():
                 add_chunk(i)
 
-            pass_on(i - LAG * blk, has_low, has_high, r_copy, zr, ro)
-            pass_on(i - LAG * (count - 1 - blk), has_high, has_low, l_copy, zl, lo)
-
-        @pl.loop(0, blocks)
-        def _(j):
-            for r, total in finish(j, 1 - sub):
-                stage[j, r * TILE:(r + 1) * TILE] = total
-            out_copy(j).start()
-
-        @pl.loop(0, blocks)
-        def _(j):
-            for r, total in finish(j, sub):
-                out[j, r * TILE:(r + 1) * TILE] = total
-
-        @pl.loop(chunks - SLOTS, chunks)
+            c = i - SKEW * blk
+
+            @pl.when((c >= 0) & (c < chunks))
+            def _():
+                pass_on(c, has_low, has_high, blk + 1)
+
+        finish(has_low, has_high, has_high, blk + 1)
+
+        @pl.loop(0, chunks)
         def _(c):
-            @pl.when(has_high)
-            def _():
-                r_copy(c).wait_send()
-
-            @pl.when(has_low)
-            def _():
-                l_copy(c).wait_send()
-
-        @pl.loop(0, blocks)
-        def _(j):
-            out_copy(j).wait_send()
+            t_copy(c).wait_send()
 
     @pl.when(jnp.logical_not(owner))
     def _():
-        @pl.loop(0, blocks)
-        def _(j):
-            out_copy(j).wait_recv()
-            out[j] = got[j]
+        @pl.loop(0, chunks + AHEAD)
+        def _(i):
+            @pl.when(i < chunks)
+            def _():
+                send_chunk(i)
+
+            @pl.when(i >= AHEAD)
+            def _():
+                t_copy(i - AHEAD).wait_recv()
+                pass_on(i - AHEAD, has_high, has_low, blk - 1)
+
+        finish(has_high, has_low, has_low, blk - 1)
 
     @pl.loop(0, pairs)
     def _(p):
-        left_remote(p).wait_send()
+        done_copy(p).wait_send()
 
     for h in range(per_half):
 
@@ -328,11 +345,9 @@
             pltpu.VMEM((op_count // 2, packed, TILE, piece), bf16),
             pltpu.VMEM((op_count - 1, packed, TILE, piece), bf16),
             pltpu.VMEM((packed, TILE, piece), bf16),
-            pltpu.VMEM((packed, TILE, piece), bf16),
             pltpu.VMEM((SLOTS, GROUP, TILE, piece), bf16),
-            pltpu.VMEM((SLOTS, GROUP, TILE, piece), bf16),
-            pltpu.VMEM((blocks, half, piece), jnp.float32),
-            pltpu.VMEM((blocks, half, piece), jnp.float32),
+            pltpu.VMEM((blocks, half, piece), bf16),
+            pltpu.VMEM((blocks, half, piece), bf16),
             pltpu.SMEM((pairs,), jnp.int32),
             pltpu.SMEM((targets,), jnp.int32),
             pltpu.SMEM((targets,), jnp.int32),
@@ -360,7 +375,7 @@
             collective_id=0, has_side_effects=True, vmem_limit_bytes=60 * 2**20
         ),
         cost_estimate=pl.CostEstimate(
-            flops=6 * pairs * half * width * width * 2,
+            flops=4 * pairs * half * width * width * 2,
             bytes_accessed=2 * left_ops.size * 2 + 2 * wavefunction.size,
             transcendentals=0,
         ),

time: 78.7 us -> 64.6 us (0.82)
  Pallas kernels: 76.1 us -> 61.9 us
    pallas_call x1, Pallas kernels: 76.1 us -> 61.9 us  [local(): pl.pallas_call(functools.partial(kernel, count, op_count, chunks), out_sh...]
where the time goes in v3:
time: 64.6 us; the launch traced here: 64.2 us
  Pallas kernels  61.9 us (96%)
  local copies, waits for them, and re-layouts  2.29 us (4%)
    pallas_call x1, Pallas kernels, local(): pl.pallas_call(functools.partial(kernel, count, op_count, chunks), out_sh...  61.9 us
    unnamed x1, local copies, waits for them, and re-layouts  2.29 us

profile of v3, /device:TPU:0, one launch (start us, length us, event | category | flops | bytes accessed | tf_op | source)
XLA Modules:
  0.0 64.2 jit_solution(17165229050876844156)
XLA Ops:
  0.0 61.9 %shard_map.82 = f32[4,256,256]{2,1,0:T(8,128)} custom-call(bf16[4,256,512]{2,1,0:T(8,128)(2,1)} %wave_hbm.1, bf16[16,256,512]{2,1,0:T(8,128)(2,1)} %left_hbm.1, bf16[16,256,512]{2,1,0:T(8,128)(2,1)} %right_hbm.1, s32[16]{0:T(128)} %src.1, s32[16]{0:T(128)} %bitcast.1, s32[16]{0:T(128)} %dst_local.1, s32[16]{0:T(128)} %row_counts.1, s32[16]{0:T(128)} %col_counts.1), custom_call_target="tpu_custom_call" | custom-call | flops 8589934592 | bytes 9437184 | tf_op jit(solution)/shard_map/pallas_call | solution.py:335
  61.9 2.3 %copy.10 = f32[4,256,256]{2,1,0:T(8,128)} copy(f32[4,256,256]{2,1,0:T(8,128)} %shard_map.82) | data formatting | bytes 2097152

commit v4 on v3

--- a/solution.py
+++ b/solution.py
@@ -10,11 +10,11 @@
 MESH = pl.DeviceIdType.MESH
 
 
-TILE = 32
+TILE = 16
 GROUP = 8
-SKEW = 3
-AHEAD = 10
-SLOTS = 4
+SKEW = 6
+AHEAD = 20
+SLOTS = 8
 
 
 def kernel(
@@ -46,6 +46,9 @@
     @pl.loop(0, pairs)
     def _(p):
         left_copy(p).start()
+
+    @pl.loop(0, pairs)
+    def _(p):
         right_copy(p).start()
 
     barrier = pltpu.get_barrier_semaphore()
@@ -132,10 +135,14 @@
     def _(p):
         right_copy(p).wait()
         done_copy(p).wait_recv()
-        product = lax.dot_general(
-            done[p], right[p], (((1,), (1,)), ((), ())), preferred_element_type=jnp.float32
-        ).astype(jnp.bfloat16)
-        runs[p + 1] = product.astype(jnp.float32).reshape(runs.shape[1:]) + runs[prev[p]]
+        for side in range(2):
+            product = lax.dot_general(
+                done[p, side * half:(side + 1) * half], right[p], (((1,), (1,)), ((), ())),
+                preferred_element_type=jnp.float32,
+            ).astype(jnp.bfloat16)
+            part = product.astype(jnp.float32).reshape((half // TILE,) + runs.shape[2:])
+            at = pl.ds(side * (half // TILE), half // TILE)
+            runs[p + 1, at] = part + runs[prev[p], at]
 
     def chunk_tiles(c):
         return pl.ds(c * GROUP, GROUP)

time: 64.6 us -> 63 us (0.975)
  Pallas kernels: 61.9 us -> 59.9 us
    pallas_call x1, Pallas kernels: 61.9 us -> 59.9 us  [local(): pl.pallas_call(functools.partial(kernel, count, op_count, chunks), out_sh...]
where the time goes in v4:
time: 63 us; the launch traced here: 62.2 us
  Pallas kernels  59.9 us (95%)
  local copies, waits for them, and re-layouts  2.29 us (4%)
    pallas_call x1, Pallas kernels, local(): pl.pallas_call(functools.partial(kernel, count, op_count, chunks), out_sh...  59.9 us
    unnamed x1, local copies, waits for them, and re-layouts  2.29 us

profile of v4, /device:TPU:0, one launch (start us, length us, event | category | flops | bytes accessed | tf_op | source)
XLA Modules:
  0.0 62.2 jit_solution(12376676290504426929)
XLA Ops:
  0.0 59.9 %shard_map.82 = f32[4,256,256]{2,1,0:T(8,128)} custom-call(bf16[4,256,512]{2,1,0:T(8,128)(2,1)} %wave_hbm.1, bf16[16,256,512]{2,1,0:T(8,128)(2,1)} %left_hbm.1, bf16[16,256,512]{2,1,0:T(8,128)(2,1)} %right_hbm.1, s32[16]{0:T(128)} %src.1, s32[16]{0:T(128)} %bitcast.1, s32[16]{0:T(128)} %dst_local.1, s32[16]{0:T(128)} %row_counts.1, s32[16]{0:T(128)} %col_counts.1), custom_call_target="tpu_custom_call" | custom-call | flops 8589934592 | bytes 9437184 | tf_op jit(solution)/shard_map/pallas_call | solution.py:342
  59.9 2.3 %copy.10 = f32[4,256,256]{2,1,0:T(8,128)} copy(f32[4,256,256]{2,1,0:T(8,128)} %shard_map.82) | data formatting | bytes 2097152

commit v5 on v4

--- a/solution.py
+++ b/solution.py
@@ -14,7 +14,6 @@
 GROUP = 8
 SKEW = 6
 AHEAD = 20
-SLOTS = 8
 
 
 def kernel(
@@ -99,15 +98,21 @@
         tiles[t] = lax.div(row_counts[t] + (TILE - 1), TILE)
         first[t + 1] = first[t] + tiles[t]
 
+    gap = chunks * GROUP - first[targets]
+
+    @pl.loop(targets // 2, targets + 1)
+    def _(t):
+        first[t] = first[t] + gap
+
     tile_of[0] = 0
     tile_row[0] = 0
 
     @pl.loop(0, chunks * GROUP)
     def _(k):
         t, r = tile_of[k], tile_row[k]
-        over = r + 1 >= tiles[t]
+        over = k + 1 >= first[t + 1]
         tile_of[k + 1] = jnp.where(over, jnp.minimum(t + 1, targets - 1), t)
-        tile_row[k + 1] = jnp.where(over, 0, r + 1)
+        tile_row[k + 1] = jnp.where(over, 0, jnp.minimum(r + 1, jnp.maximum(tiles[t] - 1, 0)))
         tile_run[k] = last[t]
 
     runs[0] = jnp.zeros(runs.shape[1:], jnp.float32)
@@ -172,7 +177,7 @@
 
     def z_copy(c, to):
         return pltpu.make_async_remote_copy(
-            src_ref=zout.at[lax.rem(c, SLOTS)], dst_ref=zin.at[chunk_tiles(c)],
+            src_ref=zout.at[chunk_tiles(c)], dst_ref=zin.at[chunk_tiles(c)],
             send_sem=z_send.at[c], recv_sem=z_recv.at[c],
             device_id={"blk": to}, device_id_type=MESH,
         )
@@ -207,6 +212,18 @@
             xr[0, k] = total.astype(xr.dtype)
         t_copy(c).start()
 
+    def turn(i):
+        return jnp.where(lax.rem(i, 2) == 0, chunks - 1 - i // 2, i // 2)
+
+    share = blocks * 2 * half // TILE
+
+    def goes_up(c, at):
+        kept = (c + 1) * GROUP > chunks * GROUP - (count - 1 - at) * share
+        return (at >= 0) & (at < count - 1) & ((at + 1 < count // 2) | kept)
+
+    def goes_down(c, at):
+        return (at > 0) & (at < count) & ((at > count // 2) | (c * GROUP < at * share))
+
     def pass_on(c, has_in, has_out, to):
         @pl.when(has_in)
         def _():
@@ -214,24 +231,20 @@
 
         @pl.when(has_out)
         def _():
-            @pl.when(c >= SLOTS)
-            def _():
-                z_copy(c - SLOTS, to).wait_send()
-
             @pl.when(has_in)
             def _():
-                zout[lax.rem(c, SLOTS)] = (
+                zout[chunk_tiles(c)] = (
                     xr[0, chunk_tiles(c)].astype(jnp.float32)
                     + zin[chunk_tiles(c)].astype(jnp.float32)
                 ).astype(zout.dtype)
 
             @pl.when(jnp.logical_not(has_in))
             def _():
-                zout[lax.rem(c, SLOTS)] = xr[0, chunk_tiles(c)]
+                zout[chunk_tiles(c)] = xr[0, chunk_tiles(c)]
 
             z_copy(c, to).start()
 
-    def finish(has_in, has_got, has_out, to):
+    def finish(has_in, has_got, sent, to):
         def tile(j, row):
             return jnp.minimum(first[blk * blocks + j] + row, chunks * GROUP - 1)
 
@@ -270,30 +283,31 @@
             def _(j):
                 out_copy(j).wait_send()
 
-        @pl.when(has_out)
-        def _():
-            @pl.loop(chunks - SLOTS, chunks)
-            def _(c):
+        @pl.loop(0, chunks)
+        def _(c):
+            @pl.when(sent(c, blk))
+            def _():
                 z_copy(c, to).wait_send()
 
     @pl.when(owner)
     def _():
         if op_count > 2:
-            pl.loop(0, chunks)(send_chunk)
+            pl.loop(0, chunks)(lambda i: send_chunk(turn(i)))
 
         @pl.loop(0, chunks + SKEW * (count - 1))
         def _(i):
             @pl.when(i < chunks)
             def _():
-                add_chunk(i)
-
-            c = i - SKEW * blk
-
-            @pl.when((c >= 0) & (c < chunks))
-            def _():
-                pass_on(c, has_low, has_high, blk + 1)
-
-        finish(has_low, has_high, has_high, blk + 1)
+                add_chunk(turn(i))
+
+            back = i - SKEW * blk
+
+            @pl.when((back >= 0) & (back < chunks))
+            def _():
+                c = turn(back)
+                pass_on(c, goes_up(c, blk - 1), goes_up(c, blk), blk + 1)
+
+        finish(has_low, has_high, goes_up, blk + 1)
 
         @pl.loop(0, chunks)
         def _(c):
@@ -305,14 +319,15 @@
         def _(i):
             @pl.when(i < chunks)
             def _():
-                send_chunk(i)
+                send_chunk(turn(i))
 
             @pl.when(i >= AHEAD)
             def _():
-                t_copy(i - AHEAD).wait_recv()
-                pass_on(i - AHEAD, has_high, has_low, blk - 1)
-
-        finish(has_high, has_low, has_low, blk - 1)
+                c = turn(i - AHEAD)
+                t_copy(c).wait_recv()
+                pass_on(c, goes_down(c, blk + 1), goes_down(c, blk), blk - 1)
+
+        finish(has_high, has_low, goes_down, blk - 1)
 
     @pl.loop(0, pairs)
     def _(p):
@@ -352,7 +367,7 @@
             pltpu.VMEM((op_count // 2, packed, TILE, piece), bf16),
             pltpu.VMEM((op_count - 1, packed, TILE, piece), bf16),
             pltpu.VMEM((packed, TILE, piece), bf16),
-            pltpu.VMEM((SLOTS, GROUP, TILE, piece), bf16),
+            pltpu.VMEM((packed, TILE, piece), bf16),
             pltpu.VMEM((blocks, half, piece), bf16),
             pltpu.VMEM((blocks, half, piece), bf16),
             pltpu.SMEM((pairs,), jnp.int32),

time: 63 us -> 61.6 us (0.978)
  Pallas kernels: 59.9 us -> 59.1 us
    pallas_call x1, Pallas kernels: 59.9 us -> 59.1 us  [local(): pl.pallas_call(functools.partial(kernel, count, op_count, chunks), out_sh...]
where the time goes in v5:
time: 61.6 us; the launch traced here: 61.4 us
  Pallas kernels  59.1 us (96%)
  local copies, waits for them, and re-layouts  2.29 us (4%)
    pallas_call x1, Pallas kernels, local(): pl.pallas_call(functools.partial(kernel, count, op_count, chunks), out_sh...  59.1 us
    unnamed x1, local copies, waits for them, and re-layouts  2.29 us

profile of v5, /device:TPU:0, one launch (start us, length us, event | category | flops | bytes accessed | tf_op | source)
XLA Modules:
  0.0 61.4 jit_solution(10160804018861945851)
XLA Ops:
  0.0 59.1 %shard_map.82 = f32[4,256,256]{2,1,0:T(8,128)} custom-call(bf16[4,256,512]{2,1,0:T(8,128)(2,1)} %wave_hbm.1, bf16[16,256,512]{2,1,0:T(8,128)(2,1)} %left_hbm.1, bf16[16,256,512]{2,1,0:T(8,128)(2,1)} %right_hbm.1, s32[16]{0:T(128)} %src.1, s32[16]{0:T(128)} %bitcast.1, s32[16]{0:T(128)} %dst_local.1, s32[16]{0:T(128)} %row_counts.1, s32[16]{0:T(128)} %col_counts.1), custom_call_target="tpu_custom_call" | custom-call | flops 8589934592 | bytes 9437184 | tf_op jit(solution)/shard_map/pallas_call | solution.py:357
  59.1 2.3 %copy.10 = f32[4,256,256]{2,1,0:T(8,128)} copy(f32[4,256,256]{2,1,0:T(8,128)} %shard_map.82) | data formatting | bytes 2097152
